TPU v7x, 32 devices: a whole 2x2x4 slice. The times are simulated.
32 devices in a mesh: inst: 2 (over x), space: 16 (over z, y, core).
Axes of the slice: x: 2, y: 2, z: 4, core: 2. Of those that a mesh axis runs over, the one named last changes fastest.
Arguments:
- state: float32 [2, 5, 64, 8192], P('inst', None, None, 'space'), may hold values from -6 to 6
- metric: float32 [8192], P('space'), may hold values from 1 to 4
- jacobians: float32 [3, 5, 5], replicated, may hold values from -2.5 to 2.5
- dissipation: float32 [1], replicated, may hold values from 0.5 to 2
- omega: float32 [1], replicated, may hold values from 0.5 to 2
- rotor_angle: float32 [2], P('inst'), may hold values from -3.140625 to 3.140625
- counts: int32 [16], P('space'), may hold values from 384 to 512, as said below
- neighbours: int32 [6, 8192], P(None, 'space'), may hold values from 0 to 639, as said below
- mortar_pairs: int32 [2, 4096], P('inst', 'space'), may hold values from 0 to 4095, as said below
Outputs:
- updated: float32 [2, 5, 64, 8192], P('inst', None, None, 'space')
Inputs may be any that keep to these rules, and one draw needn't show every extreme that they name: Some index of space has all 512 slots live; live slots are the first counts ones of a device. `neighbours`: extended numbering of a device: 64 halo slots from the previous device (its slots 64 to 127), its own 512 slots, 64 from the next device (its slots 0 to 63); every entry names a live element. `mortar_pairs`: each row is a permutation; for each instance there is one device offset, the same for all devices, such that the partners of device p's 256 faces lie on devices p plus that offset and the one after it, counted cyclically.
All inputs are finite; a program needn't handle non-finite values.
Results may differ from a plain program's by a relative error of at most 0.0001.
Values sent between devices are 32-bit elements; how exact they have to be, the bound alone decides.
No kernel may reach another device: no remote copies, remote signals or barrier semaphores. Data moves between devices by JAX's collectives and lax.ppermute only.
A program may use at most 64 MiB of HBM per device.

v0:
```python
import functools
import math

import jax
import jax.numpy as jnp
import numpy as np
from jax import lax
from jax.experimental import pallas as pl
from jax.experimental.pallas import tpu as pltpu
from jax.sharding import PartitionSpec as P

RIM = 64
FIELDS = 5
MODES = 64
FACE = 16
TRACE = FIELDS * FACE
LANES = 128
COURANT = 0.5

VMEM = pl.BlockSpec(memory_space=pltpu.VMEM)
SMEM = pl.BlockSpec(memory_space=pltpu.SMEM)
ANY = pl.BlockSpec(memory_space=pl.ANY)


def gll_table():
    nodes = np.array([-1.0, -1.0 / math.sqrt(5.0), 1.0 / math.sqrt(5.0), 1.0])
    barycentric = np.array(
        [1.0 / np.prod([nodes[j] - nodes[k] for k in range(4) if k != j]) for j in range(4)]
    )
    derivative = np.zeros((4, 4))
    for i in range(4):
        for j in range(4):
            if i != j:
                derivative[i, j] = barycentric[j] / barycentric[i] / (nodes[i] - nodes[j])
        derivative[i, i] = -np.sum(derivative[i])
    return derivative


def face_nodes(face):
    direction, index = face // 2, 3 * (face % 2)
    nodes = []
    for first in range(4):
        for second in range(4):
            if direction == 0:
                nodes.append(16 * index + 4 * first + second)
            elif direction == 1:
                nodes.append(16 * first + 4 * index + second)
            else:
                nodes.append(16 * first + 4 * second + index)
    return nodes


def operator_tables():
    derivative, identity = gll_table(), np.eye(4)
    along = [
        np.kron(np.kron(derivative, identity), identity),
        np.kron(np.kron(identity, derivative), identity),
        np.kron(np.kron(identity, identity), derivative),
    ]
    tables = [-table for table in along] + [np.zeros((MODES, MODES))]
    for face in range(6):
        sign = 1.0 if face % 2 else -1.0
        for node in face_nodes(face):
            tables[face // 2][node, node] += 3.0 * sign
            tables[3][node, node] -= 3.0
    return np.stack([np.concatenate([t, t], axis=1) for t in tables]).astype(np.float32)


def spectral_values(count):
    values = {0: (count * count + 2.0) / (12.0 * count)}
    for k in range(1 - count, count):
        if k:
            parity = -1.0 if k % 2 else 1.0
            angle = math.pi * k / count
            values[k] = 0.5 * parity / math.tan(angle) + parity / (
                2.0 * count * math.sin(angle) ** 2
            )
    return values


def split(value):
    high = value.astype(jnp.bfloat16)
    low = (value - high.astype(jnp.float32)).astype(jnp.bfloat16)
    return high, low


def fetch_all(pairs, sems):
    copies = [
        pltpu.make_async_copy(source, target, sems.at[k]) for k, (source, target) in enumerate(pairs)
    ]
    for copy in copies:
        copy.start()
    return copies


def tile_of(number):
    return slice(number * LANES, (number + 1) * LANES)


def face_pieces(face):
    direction, index = face // 2, 3 * (face % 2)
    if direction == 0:
        return [(slice(0, 16), slice(16 * index, 16 * index + 16))]
    if direction == 1:
        return [
            (slice(4 * a, 4 * a + 4), slice(16 * a + 4 * index, 16 * a + 4 * index + 4))
            for a in range(4)
        ]
    return [(slice(0, 16), pl.ds(index, 16, stride=4))]


def load_trace(cells, tile, face, trace):
    for field in range(FIELDS):
        for rows, nodes in face_pieces(face):
            target = slice(field * FACE + rows.start, field * FACE + rows.stop)
            trace[tile, target, :] = cells[tile, field, nodes, :]


def choose(sources, positions):
    shape = sources[0].shape
    lane = jnp.broadcast_to(positions & (LANES - 1), shape)
    tile = jnp.broadcast_to(positions >> 7, shape)
    result = None
    for number, source in enumerate(sources):
        found = jnp.take_along_axis(source, lane, axis=1, mode="promise_in_bounds")
        result = found if result is None else jnp.where(tile == number, found, result)
    return result


def face_weight(mixing, loss, face, g, field):
    sign = 1.0 if face % 2 else -1.0
    value = (3.0 * sign) * mixing[g, face // 2, field]
    return value - 3.0 * loss[0] if g == field else value


def base_owner(pairs, plane):
    owners = (pairs // plane).astype(jnp.float32)
    lowest = jnp.min(owners, axis=1, keepdims=True).astype(jnp.int32)
    highest = jnp.max(owners, axis=1, keepdims=True).astype(jnp.int32)
    return jnp.where(highest - lowest <= 1, lowest, highest)


def prep_kernel(plane, state, pairs, rotor, far, near, shift, pairs_here, rim, tiles, sems):
    n = lax.axis_size("space")
    me = lax.axis_index("space")
    count = plane // LANES
    copies = fetch_all(
        [(pairs, pairs_here)]
        + [
            (state.at[0, :, :, pl.ds(2 * RIM + tile * LANES, LANES)], tiles.at[tile])
            for tile in range(count)
        ]
        + [(state.at[0, :, :, pl.ds(0, 2 * RIM)], rim)],
        sems,
    )
    copies[0].wait()
    shift[0] = lax.rem(jnp.max(base_owner(pairs_here[...], plane)) - me + n, n)
    for tile in range(count):
        copies[1 + tile].wait()
        for field in range(FIELDS):
            rotor[field * FACE : (field + 1) * FACE, tile_of(tile)] = tiles[
                tile, field, pl.ds(0, FACE, stride=4), :
            ]
    copies[-1].wait()
    odd = lax.rem(me, 2) == 1
    lane = lax.broadcasted_iota(jnp.int32, (MODES // 2, 2 * RIM), 1)
    pieces = [
        rim[field, 32 * half : 32 * half + 32, :] for field in range(FIELDS) for half in range(2)
    ]
    for k in range(FIELDS):
        top, bottom = pieces[k], pieces[k + FIELDS]
        head = jnp.where(lane < RIM, top, pltpu.roll(bottom, RIM, 1))
        tail = jnp.where(lane < RIM, pltpu.roll(top, RIM, 1), bottom)
        far[32 * k : 32 * k + 32, :] = jnp.where(odd, tail, head)
        near[32 * k : 32 * k + 32, :] = jnp.where(odd, head, tail)


def own_kernel(
    plane, state, neighbours, metric, jacobians, dissipation, omega, angle, counts, pairs, tables,
    tendency, outer, given, turned, weights, places,
    metric_here, mixing, loss, frequency, turn, live_count, pairs_here, table,
    matrix, cells, trace, sems,
):
    n = lax.axis_size("space")
    inst_count = lax.axis_size("inst")
    inst = lax.axis_index("inst")
    copies = fetch_all(
        [
            (jacobians, mixing),
            (dissipation, loss),
            (omega, frequency),
            (angle, turn),
            (counts, live_count),
            (metric, metric_here),
            (pairs, pairs_here),
            (tables, table),
        ],
        sems,
    )
    count = cells.shape[0]

    for tile in range(count):
        cells[tile] = state[0, :, :, tile_of(tile)]
    for face in range(6):
        for tile in range(count):
            load_trace(cells, tile, face ^ 1, trace)
        for tile in range(count):
            outer[face, tile] = choose(
                [trace[source] for source in range(count)],
                neighbours[face : face + 1, tile_of(tile)] - RIM,
            )

    for copy in copies:
        copy.wait()
    lane = lax.broadcasted_iota(jnp.int32, (1, LANES), 1)
    order = [("high", f) for f in range(FIELDS)] * 2 + [("low", f) for f in range(FIELDS)]
    order.append(("low", None))
    for g in range(FIELDS):
        for pair in range(len(order) // 2):
            (part, left), (_, right) = order[2 * pair], order[2 * pair + 1]
            block = None
            for d in range(3):
                weight = jnp.where(
                    lane < MODES, mixing[g, d, left], 0.0 if right is None else mixing[g, d, right]
                )
                term = weight * table[d]
                block = term if block is None else block + term
            if g in (left, right):
                own = lane < MODES if g == left else lane >= MODES
                block = block + jnp.where(own, loss[0], 0.0) * table[3]
            if right is None:
                block = jnp.where(lane < MODES, block, 0.0)
            high, low = split(block)
            matrix[g * MODES : (g + 1) * MODES, tile_of(pair)] = high if part == "high" else low
    high, low = split(state[0].reshape(FIELDS * MODES, state.shape[-1]))
    stacked = jnp.concatenate([high, low, high, jnp.zeros_like(high[:MODES])], axis=0)
    product = jnp.dot(matrix[...], stacked, preferred_element_type=jnp.float32)
    for tile in range(count):
        tendency[tile] = product[:, tile_of(tile)].reshape(FIELDS, MODES, LANES)

    turns = jnp.full((1, LANES), turn[0], jnp.float32)
    cosine, sine = jnp.cos(turns), jnp.sin(turns)
    for face in range(6):
        for g in range(FIELDS):
            row = (face * FIELDS + g) * FIELDS
            values = [face_weight(mixing, loss, face, g, field) for field in range(FIELDS)]
            for field in range(FIELDS):
                given[row + field : row + field + 1, :] = jnp.full((1, LANES), values[field])
            if face == 5:
                values[2], values[3] = (
                    values[2] * cosine + values[3] * sine,
                    values[3] * cosine - values[2] * sine,
                )
                for field in range(FIELDS):
                    row = g * FIELDS + field
                    turned[row : row + 1, :] = jnp.broadcast_to(values[field], (1, LANES))

    spectral = spectral_values(inst_count)
    scale = metric_here[...]
    step = COURANT / (scale * loss[0] + frequency[0])
    live = lax.broadcasted_iota(jnp.int32, scale.shape, 1) < live_count[0]
    step = jnp.where(live, step, 0.0)
    weights[0:1, :] = step * scale
    weights[1:2, :] = jnp.where(live, 1.0, 0.0) - step * (frequency[0] * spectral[0])
    for away in range(1, inst_count):
        value = jnp.where(inst + away < inst_count, spectral[-away], spectral[inst_count - away])
        weights[away + 1 : away + 2, :] = -step * (frequency[0] * value)

    place = pairs_here[...] - base_owner(pairs_here[...], plane) * plane
    places[...] = jnp.where(place < 0, place + n * plane, place)


def halo_kernel(
    plane, state, neighbours, weights, given, tendency, outer, from_far, from_near,
    partial, rim, trace,
):
    count = partial.shape[0]
    elems = state.shape[-1]
    odd = lax.rem(lax.axis_index("space"), 2) == 1
    half_lane = lax.broadcasted_iota(jnp.int32, (MODES // 2, 2 * RIM), 1)
    for k in range(2 * FIELDS):
        field, half = k // 2, k % 2
        piece = pl.ds(32 * (k % FIELDS), 32)
        left = jnp.where(odd, from_near[piece, :], from_far[piece, :])
        right = jnp.where(odd, from_far[piece, :], from_near[piece, :])
        if k < FIELDS:
            right = pltpu.roll(right, RIM, 1)
        else:
            left = pltpu.roll(left, RIM, 1)
        rim[0, field, 32 * half : 32 * half + 32, :] = jnp.where(half_lane < RIM, left, right)
    lane = lax.broadcasted_iota(jnp.int32, (1, LANES), 1)

    partial[...] = tendency[...]
    for face in range(6):
        load_trace(rim, 0, face ^ 1, trace)
        for tile in range(count):
            number = neighbours[face : face + 1, tile_of(tile)]
            previous = number < RIM
            remote = previous | (number >= RIM + elems)
            found = choose([trace[0]], jnp.where(previous, number, number - elems))
            found = jnp.where(remote, found, outer[face, tile])
            if face == 5:
                column = lane + tile * LANES
                sliding = (column >= 2 * RIM) & (column < 2 * RIM + plane)
                found = jnp.where(sliding, 0.0, found)
            lift(partial, tile, face, mix(given, face, found), 1.0)
    for tile in range(count):
        scale, keep = weights[0:1, tile_of(tile)], weights[1:2, tile_of(tile)]
        partial[tile] = keep * state[0, :, :, tile_of(tile)] + scale * partial[tile]


def mix(given, face, found):
    mixed = []
    for g in range(FIELDS):
        total = None
        for field in range(FIELDS):
            row = (face * FIELDS + g) * FIELDS + field
            term = given[row : row + 1, :] * found[field * FACE : (field + 1) * FACE]
            total = term if total is None else total + term
        mixed.append(total)
    return mixed


def lift(cells, tile, face, mixed, scale):
    for g in range(FIELDS):
        change = scale * mixed[g]
        for rows, nodes in face_pieces(face):
            cells[tile, g, nodes, :] = cells[tile, g, nodes, :] - change[rows]


def final_kernel(plane, partial, weights, turned, places, first, second, *refs):
    inst_count = lax.axis_size("inst")
    others, (result, buffer, sems) = refs[: inst_count - 1], refs[inst_count - 1 :]
    count = buffer.shape[0]
    start, stop = 2 * RIM // LANES, (2 * RIM + plane) // LANES
    copies = []
    for tile in [*range(start, stop), *range(start), *range(stop, count)]:
        for field in range(FIELDS):
            total = partial[tile, field]
            for away in range(1, inst_count):
                row = weights[away + 1 : away + 2, tile_of(tile)]
                total = total + row * others[away - 1][0, field, :, tile_of(tile)]
            buffer[tile, field] = total
        if start <= tile < stop:
            positions = places[:, tile_of(tile - start)]
            found = choose(
                [
                    block[:, tile_of(source)]
                    for block in (first, second)
                    for source in range(plane // LANES)
                ],
                positions,
            )
            lift(buffer, tile, 5, mix(turned, 0, found), weights[0:1, tile_of(tile)])
        copies.append(
            pltpu.make_async_copy(
                buffer.at[tile], result.at[0, :, :, pl.ds(tile * LANES, LANES)], sems.at[tile]
            )
        )
        copies[-1].start()
    for copy in copies:
        copy.wait()


def shards(
    state, metric, jacobians, dissipation, omega, rotor_angle, counts, neighbours, mortar_pairs
):
    elems = state.shape[-1]
    tiles = elems // LANES
    plane = mortar_pairs.shape[-1]
    n = lax.axis_size("space")
    inst_count = lax.axis_size("inst")
    f32 = jnp.float32
    shape = jax.ShapeDtypeStruct
    mixing = jnp.transpose(jacobians, (1, 0, 2))
    sems = pltpu.SemaphoreType.DMA
    scalar = pltpu.SMEM((1,), f32)
    params = pltpu.CompilerParams(vmem_limit_bytes=32 * 2**20)

    others = [
        lax.ppermute(state, "inst", [((i + away) % inst_count, i) for i in range(inst_count)])
        for away in range(1, inst_count)
    ]

    rotor, far, near, shift = pl.pallas_call(
        functools.partial(prep_kernel, plane),
        out_shape=(
            shape((TRACE, plane), f32),
            shape((FIELDS * MODES // 2, 2 * RIM), f32),
            shape((FIELDS * MODES // 2, 2 * RIM), f32),
            shape((1,), jnp.int32),
        ),
        in_specs=[ANY, ANY],
        out_specs=(VMEM, VMEM, VMEM, SMEM),
        scratch_shapes=[
            pltpu.VMEM((1, plane), jnp.int32),
            pltpu.VMEM((FIELDS, MODES, 2 * RIM), f32),
            pltpu.VMEM((plane // LANES, FIELDS, MODES, LANES), f32),
            sems((plane // LANES + 2,)),
        ],
        name="prep",
    )(state, mortar_pairs)

    def fetch(away, block):
        if away == 0:
            return block
        return lax.ppermute(block, "space", [((i + away) % n, i) for i in range(n)])

    ends = [(i, (i + 1) % n) for i in range(1, n, 2)]
    middles = [(i, i + 1) for i in range(0, n, 2)]

    def swap(pairs, block):
        return lax.ppermute(block, "space", pairs + [(j, i) for i, j in pairs])

    def branch(away, rotor, far, near, *operands):
        first = fetch(away, rotor)
        from_far, from_near = swap(ends, far), swap(middles, near)
        own = pl.pallas_call(
            functools.partial(own_kernel, plane),
            out_shape=(
                shape((tiles, FIELDS, MODES, LANES), f32),
                shape((6, tiles, TRACE, LANES), f32),
                shape((6 * FIELDS * FIELDS, LANES), f32),
                shape((FIELDS * FIELDS, LANES), f32),
                shape((inst_count + 1, elems), f32),
                shape((1, plane), jnp.int32),
            ),
            in_specs=[VMEM, VMEM] + [ANY] * 8,
            out_specs=(VMEM,) * 6,
            scratch_shapes=[
                pltpu.VMEM((1, elems), f32),
                pltpu.SMEM((FIELDS, 3, FIELDS), f32),
                scalar,
                scalar,
                scalar,
                pltpu.SMEM((1,), jnp.int32),
                pltpu.VMEM((1, plane), jnp.int32),
                pltpu.VMEM((4, MODES, LANES), f32),
                pltpu.VMEM((FIELDS * MODES, 8 * LANES), jnp.bfloat16),
                pltpu.VMEM((tiles, FIELDS, MODES, LANES), f32),
                pltpu.VMEM((tiles, TRACE, LANES), f32),
                sems((8,)),
            ],
            compiler_params=params,
            cost_estimate=pl.CostEstimate(
                flops=2**31, bytes_accessed=2**22, transcendentals=0
            ),
            name="own",
        )(*operands)
        return first, from_far, from_near, own

    first, from_far, from_near, own = lax.switch(
        shift[0],
        [functools.partial(branch, away) for away in range(n)],
        rotor, far, near, state, neighbours, metric.reshape(1, elems), mixing, dissipation, omega,
        rotor_angle, counts, mortar_pairs, jnp.asarray(operator_tables()),
    )
    tendency, outer, given, turned, weights, places = own
    second = fetch(1, first)

    partial = pl.pallas_call(
        functools.partial(halo_kernel, plane),
        out_shape=shape((tiles, FIELDS, MODES, LANES), f32),
        in_specs=[VMEM] * 8,
        out_specs=VMEM,
        scratch_shapes=[
            pltpu.VMEM((1, FIELDS, MODES, 2 * RIM), f32),
            pltpu.VMEM((1, TRACE, LANES), f32),
        ],
        compiler_params=params,
        cost_estimate=pl.CostEstimate(flops=2**31, bytes_accessed=2**22, transcendentals=0),
        name="halo",
    )(state, neighbours, weights, given, tendency, outer, from_far, from_near)

    return pl.pallas_call(
        functools.partial(final_kernel, plane),
        out_shape=shape(state.shape, f32),
        in_specs=[VMEM] * (5 + inst_count),
        out_specs=ANY,
        scratch_shapes=[
            pltpu.VMEM((tiles, FIELDS, MODES, LANES), f32),
            sems((tiles,)),
        ],
        compiler_params=params,
        name="final",
    )(partial, weights, turned, places, first, second, *others)


def solution(mesh):
    return jax.shard_map(
        shards,
        mesh=mesh,
        in_specs=(
            P("inst", None, None, "space"),
            P("space"),
            P(),
            P(),
            P(),
            P("inst"),
            P("space"),
            P(None, "space"),
            P("inst", "space"),
        ),
        out_specs=P("inst", None, None, "space"),
        check_vma=False,
    )
```

profile of v0, /device:TPU:0, one launch (start us, length us, event | category | flops | bytes accessed | tf_op | source)
XLA Modules:
  0.0 21.4 jit_solution(17257399063877009496)
XLA Ops:
  0.0 0.0 copy-start
  0.0 2.9 %collective-permute-start.48 = (f32[1,5,64,512]{3,2,1,0:T(8,128)}, f32[1,5,64,512]{3,2,1,0:T(8,128)S(1)}, u32[]{:S(2)}, u32[]{:S(2)}) collective-permute-start(f32[1,5,64,512]{3,2,1,0:T(8,128)} %state.3), channel_id=1, source_target_pairs={{16,0},{0,16},{17,1},{1,17},{18,2},{2,18},{19,3},{3,19},{20,4},{4,... | collective-permute-start | bytes 1966088 | tf_op jit(solution)/shard_map/ppermute | solution.py:381
  2.9 1.6 %prep.1 = (f32[80,256]{1,0:T(8,128)S(1)}, f32[160,128]{1,0:T(8,128)S(1)}, f32[160,128]{1,0:T(8,128)S(1)}, s32[1]{0:T(128)}) custom-call(f32[1,5,64,512]{3,2,1,0:T(8,128)} %state.3, s32[1,256]{1,0:T(1,128)} %pairs.1), custom_call_target="tpu_custom_call" | custom-call | tf_op jit(solution)/shard_map/prep/pallas_call | solution.py:385
  4.6 0.0 copy-start.2
  4.6 0.0 copy-start.1
  5.3 0.0 copy-done
  5.3 0.0 copy-done.2
  5.3 0.0 copy-done.1
  5.3 10.0 %conditional.1 = (f32[80,256]{1,0:T(8,128)S(1)}, f32[160,128]{1,0:T(8,128)}, f32[160,128]{1,0:T(8,128)}, f32[4,5,64,128]{3,2,1,0:T(8,128)S(1)}, f32[6,4,80,128]{...) conditional(s32[]{:T(128)} %bitcast, ...), branch_computations={%region_0.0_spmd, %region_1.0_spmd, %region_2.0_spmd, %region_3.0_... | conditional | flops 2147483648 | bytes 5350824 | solution.py:452
  5.5 2.7 %collective-permute-start.23 = (f32[80,256]{1,0:T(8,128)S(1)}, f32[80,256]{1,0:T(8,128)S(1)}, u32[]{:S(2)}, u32[]{:S(2)}) collective-permute-start(f32[80,256]{1,0:T(8,128)S(1)} %get-tuple-element.573), channel_id=1, source_target_pairs={{8,0},{9,1},{10,2},{11,3},{12,4},{13,5},{14,6},{15,7},{0,8},{1,9},... | collective-permute-start | bytes 245768 | tf_op jit(solution)/shard_map/cond/branch_8_fun/ppermute | solution.py:407
  8.2 0.0 copy-start.11
  8.2 1.2 %collective-permute-start.24 = (f32[160,128]{1,0:T(8,128)S(1)}, f32[160,128]{1,0:T(8,128)}, u32[]{:S(2)}, u32[]{:S(2)}) collective-permute-start(f32[160,128]{1,0:T(8,128)S(1)} %get-tuple-element.574), channel_id=1, source_target_pairs={{1,2},{3,4},{5,6},{7,8},{9,10},{11,12},{13,14},{15,0},{2,1},{4,3},... | collective-permute-start | bytes 245768 | tf_op jit(solution)/shard_map/cond/branch_8_fun/ppermute | solution.py:413
  9.4 0.4 %collective-permute-start.25 = (f32[160,128]{1,0:T(8,128)S(1)}, f32[160,128]{1,0:T(8,128)}, u32[]{:S(2)}, u32[]{:S(2)}) collective-permute-start(f32[160,128]{1,0:T(8,128)S(1)} %get-tuple-element.575), channel_id=1, source_target_pairs={{0,1},{2,3},{4,5},{6,7},{8,9},{10,11},{12,13},{14,15},{1,0},{3,2},... | collective-permute-start | bytes 245768 | tf_op jit(solution)/shard_map/cond/branch_8_fun/ppermute | solution.py:413
  9.8 0.0 copy-done.11
  9.8 0.7 %copy-done.27 = f32[1,512]{1,0:T(1,128)S(1)} copy-done((f32[1,512]{1,0:T(1,128)S(1)}, f32[1,512]{1,0:T(1,128)}, u32[]{:S(2)}) %copy-start.27) | copy-done | bytes 2072 | tf_op jit(solution)/shard_map/cond
  10.5 4.8 %own.24 = (f32[4,5,64,128]{3,2,1,0:T(8,128)S(1)}, f32[6,4,80,128]{3,2,1,0:T(8,128)S(1)}, f32[150,128]{1,0:T(8,128)S(1)}, f32[25,128]{1,0:T(8,128)S(1)}, f32[3,512]{1,0:T(4,128)S(1)}, /*index=5*/s32[1,256]{1,0:T(1,128)S(1)}) custom-call(f32[1,5,64,512]{3,2,1,0:T(8,128)S(1)} %get-tuple-element.576.state, s32[6,512]{1,0:T(8,128)S(1)} %get-tuple-element.577.neighbours, ...), custom_call_target="tpu_custom_call" | custom-call | flops 2147483648 | bytes 4194304 | tf_op jit(solution)/shard_map/cond/branch_8_fun/own/pallas_call | solution.py:418
  15.3 0.0 collective-permute-done.23
  15.3 0.0 collective-permute-done.24
  15.3 0.0 collective-permute-done.25
  15.3 2.9 %collective-permute-start.47 = (f32[80,256]{1,0:T(8,128)S(1)}, f32[80,256]{1,0:T(8,128)S(1)}, u32[]{:S(2)}, u32[]{:S(2)}) collective-permute-start(f32[80,256]{1,0:T(8,128)S(1)} %get-tuple-element.750.first), channel_id=1, source_target_pairs={{1,0},{2,1},{3,2},{4,3},{5,4},{6,5},{7,6},{8,7},{9,8},{10,9},{11,1... | collective-permute-start | bytes 245768 | tf_op jit(solution)/shard_map/ppermute | solution.py:407
  18.2 1.7 %halo.1.partial = f32[4,5,64,128]{3,2,1,0:T(8,128)S(1)} custom-call(f32[1,5,64,512]{3,2,1,0:T(8,128)S(1)} %copy-done, s32[6,512]{1,0:T(8,128)S(1)} %copy-done.2, f32[3,512]{1,0:T(4,128)S(1)} %get-tuple-element.742.weights, f32[150,128]{1,0:T(8,128)S(1)} %get-tuple-element.743.given, f32[4,5,64,128]{3,2,1,0:T(8,128)S(1)} %get-tuple-element.744.tendency, ...), custom_call_target="tpu_custom_call" | custom-call | flops 2147483648 | bytes 4194304 | tf_op jit(solution)/shard_map/halo/pallas_call | solution.py:461
  19.9 0.4 %collective-permute-done.47.second = f32[80,256]{1,0:T(8,128)S(1)} collective-permute-done((f32[80,256]{1,0:T(8,128)S(1)}, f32[80,256]{1,0:T(8,128)S(1)}, u32[]{:S(2)}, u32[]{:S(2)}) %collective-permute-start.47) | collective-permute-done | bytes 81952 | tf_op jit(solution)/shard_map/ppermute | solution.py:407
  20.3 0.0 collective-permute-done.48.refs_0_
  20.3 1.0 %final.1 = f32[1,5,64,512]{3,2,1,0:T(8,128)} custom-call(f32[4,5,64,128]{3,2,1,0:T(8,128)S(1)} %halo.1.partial, f32[3,512]{1,0:T(4,128)S(1)} %get-tuple-element.742.weights, f32[25,128]{1,0:T(8,128)S(1)} %get-tuple-element.748.turned, s32[1,256]{1,0:T(1,128)S(1)} %get-tuple-element.749.places, f32[80,256]{1,0:T(8,128)S(1)} %get-tuple-element.750.first, ...), custom_call_target="tpu_custom_call" | custom-call | tf_op jit(solution)/shard_map/final/pallas_call | solution.py:475
  (2 shorter events, 0.0 us)
Async XLA Ops:
  0.0 5.3 %copy-start = (f32[1,5,64,512]{3,2,1,0:T(8,128)S(1)}, f32[1,5,64,512]{3,2,1,0:T(8,128)}, u32[]{:S(2)}) copy-start(f32[1,5,64,512]{3,2,1,0:T(8,128)} %state.3) | copy-start | bytes 1966084
  0.0 20.3 %collective-permute-start.48 = (f32[1,5,64,512]{3,2,1,0:T(8,128)}, f32[1,5,64,512]{3,2,1,0:T(8,128)S(1)}, u32[]{:S(2)}, u32[]{:S(2)}) collective-permute-start(f32[1,5,64,512]{3,2,1,0:T(8,128)} %state.3), channel_id=1, source_target_pairs={{16,0},{0,16},{17,1},{1,17},{18,2},{2,18},{19,3},{3,19},{20,4},{4,... | collective-permute-start | bytes 1966088 | tf_op jit(solution)/shard_map/ppermute | solution.py:381
  4.6 0.7 %copy-start.2 = (s32[6,512]{1,0:T(8,128)S(1)}, s32[6,512]{1,0:T(8,128)}, u32[]{:S(2)}) copy-start(s32[6,512]{1,0:T(8,128)} %neighbours.1) | copy-start | bytes 36868
  4.6 0.7 %copy-start.1 = (s32[1,256]{1,0:T(1,128)S(1)}, s32[1,256]{1,0:T(1,128)}, u32[]{:S(2)}) copy-start(s32[1,256]{1,0:T(1,128)} %pairs.1) | copy-start | bytes 3076
  5.5 9.7 %collective-permute-start.23 = (f32[80,256]{1,0:T(8,128)S(1)}, f32[80,256]{1,0:T(8,128)S(1)}, u32[]{:S(2)}, u32[]{:S(2)}) collective-permute-start(f32[80,256]{1,0:T(8,128)S(1)} %get-tuple-element.573), channel_id=1, source_target_pairs={{8,0},{9,1},{10,2},{11,3},{12,4},{13,5},{14,6},{15,7},{0,8},{1,9},... | collective-permute-start | bytes 245768 | tf_op jit(solution)/shard_map/cond/branch_8_fun/ppermute | solution.py:407
  8.2 1.6 %copy-start.11 = (f32[5,3,5]{2,1,0:T(4,128)S(1)}, f32[5,3,5]{2,1,0:T(4,128)}, u32[]{:S(2)}) copy-start(f32[5,3,5]{2,1,0:T(4,128)} %get-tuple-element.579.jacobians) | copy-start | bytes 904 | tf_op jit(solution)/shard_map/cond
  8.2 7.1 %collective-permute-start.24 = (f32[160,128]{1,0:T(8,128)S(1)}, f32[160,128]{1,0:T(8,128)}, u32[]{:S(2)}, u32[]{:S(2)}) collective-permute-start(f32[160,128]{1,0:T(8,128)S(1)} %get-tuple-element.574), channel_id=1, source_target_pairs={{1,2},{3,4},{5,6},{7,8},{9,10},{11,12},{13,14},{15,0},{2,1},{4,3},... | collective-permute-start | bytes 245768 | tf_op jit(solution)/shard_map/cond/branch_8_fun/ppermute | solution.py:413
  9.4 5.9 %collective-permute-start.25 = (f32[160,128]{1,0:T(8,128)S(1)}, f32[160,128]{1,0:T(8,128)}, u32[]{:S(2)}, u32[]{:S(2)}) collective-permute-start(f32[160,128]{1,0:T(8,128)S(1)} %get-tuple-element.575), channel_id=1, source_target_pairs={{0,1},{2,3},{4,5},{6,7},{8,9},{10,11},{12,13},{14,15},{1,0},{3,2},... | collective-permute-start | bytes 245768 | tf_op jit(solution)/shard_map/cond/branch_8_fun/ppermute | solution.py:413
  9.8 0.7 %copy-start.27 = (f32[1,512]{1,0:T(1,128)S(1)}, f32[1,512]{1,0:T(1,128)}, u32[]{:S(2)}) copy-start(f32[1,512]{1,0:T(1,128)} %get-tuple-element.578.metric) | copy-start | bytes 6148 | tf_op jit(solution)/shard_map/cond
  15.3 4.9 %collective-permute-start.47 = (f32[80,256]{1,0:T(8,128)S(1)}, f32[80,256]{1,0:T(8,128)S(1)}, u32[]{:S(2)}, u32[]{:S(2)}) collective-permute-start(f32[80,256]{1,0:T(8,128)S(1)} %get-tuple-element.750.first), channel_id=1, source_target_pairs={{1,0},{2,1},{3,2},{4,3},{5,4},{6,5},{7,6},{8,7},{9,8},{10,9},{11,1... | collective-permute-start | bytes 245768 | tf_op jit(solution)/shard_map/ppermute | solution.py:407
where the time goes:
time: 21.4 us
  starting transfers between devices  10.1 us (47%)
  Pallas kernels  9.07 us (42%)
  between operations  0.88 us (4%)
  local copies, waits for them, and re-layouts  0.73 us (3%)
  waiting for transfers between devices  0.38 us (2%)
  loops' own time  0.27 us (1%)
    ppermute x2, starting transfers between devices, fetch(): return lax.ppermute(block, 'space', [((i + away) % n, i) for i in range(n)])  5.52 us
    pallas_call x1, Pallas kernels, branch(): pl.pallas_call(functools.partial(own_kernel, plane), out_shape=(shape((ti...  4.75 us
    ppermute x1, starting transfers between devices, shards(): lax.ppermute(state, 'inst', [((i + away) % inst_count, i) for i in range(...  2.94 us
    pallas_call x1, Pallas kernels, shards(): pl.pallas_call(functools.partial(halo_kernel, plane), out_shape=shape((ti...  1.68 us
    pallas_call x1, Pallas kernels, shards(): pl.pallas_call(functools.partial(prep_kernel, plane), out_shape=(shape((T...  1.64 us
    ppermute x2, starting transfers between devices, swap(): return lax.ppermute(block, 'space', pairs + [(j, i) for i, j in pairs])  1.63 us
    pallas_call x1, Pallas kernels, shards(): pl.pallas_call(functools.partial(final_kernel, plane), out_shape=shape(st...  1 us
    cond x5, local copies, waits for them, and re-layouts  0.69 us
  transfers between devices with their start and end apart: 5, of which 1 were waited for; matrix products, arithmetic and copies ran while one was open for 0% of the time, Pallas kernels for 38%

commit v1 on v0

--- a/solution.py
+++ b/solution.py
@@ -125,12 +125,6 @@
         found = jnp.take_along_axis(source, lane, axis=1, mode="promise_in_bounds")
         result = found if result is None else jnp.where(tile == number, found, result)
     return result
-
-
-def face_weight(mixing, loss, face, g, field):
-    sign = 1.0 if face % 2 else -1.0
-    value = (3.0 * sign) * mixing[g, face // 2, field]
-    return value - 3.0 * loss[0] if g == field else value
 
 
 def base_owner(pairs, plane):
@@ -177,7 +171,7 @@
 
 def own_kernel(
     plane, state, neighbours, metric, jacobians, dissipation, omega, angle, counts, pairs, tables,
-    tendency, outer, given, turned, weights, places,
+    tendency, outer, frame, weights, places,
     metric_here, mixing, loss, frequency, turn, live_count, pairs_here, table,
     matrix, cells, trace, sems,
 ):
@@ -239,21 +233,9 @@
         tendency[tile] = product[:, tile_of(tile)].reshape(FIELDS, MODES, LANES)
 
     turns = jnp.full((1, LANES), turn[0], jnp.float32)
-    cosine, sine = jnp.cos(turns), jnp.sin(turns)
-    for face in range(6):
-        for g in range(FIELDS):
-            row = (face * FIELDS + g) * FIELDS
-            values = [face_weight(mixing, loss, face, g, field) for field in range(FIELDS)]
-            for field in range(FIELDS):
-                given[row + field : row + field + 1, :] = jnp.full((1, LANES), values[field])
-            if face == 5:
-                values[2], values[3] = (
-                    values[2] * cosine + values[3] * sine,
-                    values[3] * cosine - values[2] * sine,
-                )
-                for field in range(FIELDS):
-                    row = g * FIELDS + field
-                    turned[row : row + 1, :] = jnp.broadcast_to(values[field], (1, LANES))
+    frame[0:1, :] = jnp.cos(turns)
+    frame[1:2, :] = jnp.sin(turns)
+    frame[2:3, :] = jnp.full((1, LANES), 3.0 * loss[0], jnp.float32)
 
     spectral = spectral_values(inst_count)
     scale = metric_here[...]
@@ -270,10 +252,11 @@
     places[...] = jnp.where(place < 0, place + n * plane, place)
 
 
-def halo_kernel(
-    plane, state, neighbours, weights, given, tendency, outer, from_far, from_near,
-    partial, rim, trace,
+def join_kernel(
+    plane, state, neighbours, weights, frame, places, jacobians, tendency, outer,
+    from_far, from_near, first, second, partial, mixing, rim, trace, sems,
 ):
+    [copy] = fetch_all([(jacobians, mixing)], sems)
     count = partial.shape[0]
     elems = state.shape[-1]
     odd = lax.rem(lax.axis_index("space"), 2) == 1
@@ -288,70 +271,58 @@
         else:
             left = pltpu.roll(left, RIM, 1)
         rim[0, field, 32 * half : 32 * half + 32, :] = jnp.where(half_lane < RIM, left, right)
-    lane = lax.broadcasted_iota(jnp.int32, (1, LANES), 1)
-
     partial[...] = tendency[...]
+    copy.wait()
+
+    start, stop = 2 * RIM // LANES, (2 * RIM + plane) // LANES
     for face in range(6):
         load_trace(rim, 0, face ^ 1, trace)
         for tile in range(count):
-            number = neighbours[face : face + 1, tile_of(tile)]
-            previous = number < RIM
-            remote = previous | (number >= RIM + elems)
-            found = choose([trace[0]], jnp.where(previous, number, number - elems))
-            found = jnp.where(remote, found, outer[face, tile])
-            if face == 5:
-                column = lane + tile * LANES
-                sliding = (column >= 2 * RIM) & (column < 2 * RIM + plane)
-                found = jnp.where(sliding, 0.0, found)
-            lift(partial, tile, face, mix(given, face, found), 1.0)
+            if face == 5 and start <= tile < stop:
+                found = choose(
+                    [
+                        block[:, tile_of(source)]
+                        for block in (first, second)
+                        for source in range(plane // LANES)
+                    ],
+                    places[:, tile_of(tile - start)],
+                )
+                parts = [found[field * FACE : (field + 1) * FACE] for field in range(FIELDS)]
+                cosine, sine = frame[0:1, :], frame[1:2, :]
+                parts[2], parts[3] = (
+                    cosine * parts[2] - sine * parts[3],
+                    sine * parts[2] + cosine * parts[3],
+                )
+            else:
+                number = neighbours[face : face + 1, tile_of(tile)]
+                previous = number < RIM
+                remote = previous | (number >= RIM + elems)
+                found = choose([trace[0]], jnp.where(previous, number, number - elems))
+                found = jnp.where(remote, found, outer[face, tile])
+                parts = [found[field * FACE : (field + 1) * FACE] for field in range(FIELDS)]
+            for g in range(FIELDS):
+                change = -frame[2:3, :] * parts[g]
+                for field in range(FIELDS):
+                    sign = 3.0 if face % 2 else -3.0
+                    change = change + (sign * mixing[g, face // 2, field]) * parts[field]
+                for rows, nodes in face_pieces(face):
+                    partial[tile, g, nodes, :] = partial[tile, g, nodes, :] - change[rows]
     for tile in range(count):
         scale, keep = weights[0:1, tile_of(tile)], weights[1:2, tile_of(tile)]
         partial[tile] = keep * state[0, :, :, tile_of(tile)] + scale * partial[tile]
 
 
-def mix(given, face, found):
-    mixed = []
-    for g in range(FIELDS):
-        total = None
-        for field in range(FIELDS):
-            row = (face * FIELDS + g) * FIELDS + field
-            term = given[row : row + 1, :] * found[field * FACE : (field + 1) * FACE]
-            total = term if total is None else total + term
-        mixed.append(total)
-    return mixed
-
-
-def lift(cells, tile, face, mixed, scale):
-    for g in range(FIELDS):
-        change = scale * mixed[g]
-        for rows, nodes in face_pieces(face):
-            cells[tile, g, nodes, :] = cells[tile, g, nodes, :] - change[rows]
-
-
-def final_kernel(plane, partial, weights, turned, places, first, second, *refs):
+def final_kernel(partial, weights, *refs):
     inst_count = lax.axis_size("inst")
     others, (result, buffer, sems) = refs[: inst_count - 1], refs[inst_count - 1 :]
-    count = buffer.shape[0]
-    start, stop = 2 * RIM // LANES, (2 * RIM + plane) // LANES
     copies = []
-    for tile in [*range(start, stop), *range(start), *range(stop, count)]:
+    for tile in range(buffer.shape[0]):
         for field in range(FIELDS):
             total = partial[tile, field]
             for away in range(1, inst_count):
                 row = weights[away + 1 : away + 2, tile_of(tile)]
                 total = total + row * others[away - 1][0, field, :, tile_of(tile)]
             buffer[tile, field] = total
-        if start <= tile < stop:
-            positions = places[:, tile_of(tile - start)]
-            found = choose(
-                [
-                    block[:, tile_of(source)]
-                    for block in (first, second)
-                    for source in range(plane // LANES)
-                ],
-                positions,
-            )
-            lift(buffer, tile, 5, mix(turned, 0, found), weights[0:1, tile_of(tile)])
         copies.append(
             pltpu.make_async_copy(
                 buffer.at[tile], result.at[0, :, :, pl.ds(tile * LANES, LANES)], sems.at[tile]
@@ -402,7 +373,7 @@
     )(state, mortar_pairs)
 
     def fetch(away, block):
-        if away == 0:
+        if away % n == 0:
             return block
         return lax.ppermute(block, "space", [((i + away) % n, i) for i in range(n)])
 
@@ -413,20 +384,19 @@
         return lax.ppermute(block, "space", pairs + [(j, i) for i, j in pairs])
 
     def branch(away, rotor, far, near, *operands):
-        first = fetch(away, rotor)
+        first, second = fetch(away, rotor), fetch(away + 1, rotor)
         from_far, from_near = swap(ends, far), swap(middles, near)
         own = pl.pallas_call(
             functools.partial(own_kernel, plane),
             out_shape=(
                 shape((tiles, FIELDS, MODES, LANES), f32),
                 shape((6, tiles, TRACE, LANES), f32),
-                shape((6 * FIELDS * FIELDS, LANES), f32),
-                shape((FIELDS * FIELDS, LANES), f32),
+                shape((8, LANES), f32),
                 shape((inst_count + 1, elems), f32),
                 shape((1, plane), jnp.int32),
             ),
             in_specs=[VMEM, VMEM] + [ANY] * 8,
-            out_specs=(VMEM,) * 6,
+            out_specs=(VMEM,) * 5,
             scratch_shapes=[
                 pltpu.VMEM((1, elems), f32),
                 pltpu.SMEM((FIELDS, 3, FIELDS), f32),
@@ -447,35 +417,39 @@
             ),
             name="own",
         )(*operands)
-        return first, from_far, from_near, own
-
-    first, from_far, from_near, own = lax.switch(
+        return first, second, from_far, from_near, own
+
+    first, second, from_far, from_near, own = lax.switch(
         shift[0],
         [functools.partial(branch, away) for away in range(n)],
         rotor, far, near, state, neighbours, metric.reshape(1, elems), mixing, dissipation, omega,
         rotor_angle, counts, mortar_pairs, jnp.asarray(operator_tables()),
     )
-    tendency, outer, given, turned, weights, places = own
-    second = fetch(1, first)
+    tendency, outer, frame, weights, places = own
 
     partial = pl.pallas_call(
-        functools.partial(halo_kernel, plane),
+        functools.partial(join_kernel, plane),
         out_shape=shape((tiles, FIELDS, MODES, LANES), f32),
-        in_specs=[VMEM] * 8,
+        in_specs=[VMEM] * 5 + [ANY] + [VMEM] * 6,
         out_specs=VMEM,
         scratch_shapes=[
+            pltpu.SMEM((FIELDS, 3, FIELDS), f32),
             pltpu.VMEM((1, FIELDS, MODES, 2 * RIM), f32),
             pltpu.VMEM((1, TRACE, LANES), f32),
+            sems((1,)),
         ],
         compiler_params=params,
         cost_estimate=pl.CostEstimate(flops=2**31, bytes_accessed=2**22, transcendentals=0),
-        name="halo",
-    )(state, neighbours, weights, given, tendency, outer, from_far, from_near)
+        name="join",
+    )(
+        state, neighbours, weights, frame, places, mixing, tendency, outer,
+        from_far, from_near, first, second,
+    )
 
     return pl.pallas_call(
-        functools.partial(final_kernel, plane),
+        final_kernel,
         out_shape=shape(state.shape, f32),
-        in_specs=[VMEM] * (5 + inst_count),
+        in_specs=[VMEM] * (1 + inst_count),
         out_specs=ANY,
         scratch_shapes=[
             pltpu.VMEM((tiles, FIELDS, MODES, LANES), f32),
@@ -483,7 +457,7 @@
         ],
         compiler_params=params,
         name="final",
-    )(partial, weights, turned, places, first, second, *others)
+    )(partial, weights, *others)
 
 
 def solution(mesh):

time: 21.4 us -> 20.8 us (0.972)
  the two profiles are of different devices: /device:TPU:0 before, /device:TPU:3 now
where the time goes in v1:
time: 20.8 us; the launch traced here: 20.5 us
  Pallas kernels  9.77 us (47%)
  starting transfers between devices  8.35 us (40%)
  local copies, waits for them, and re-layouts  1.39 us (7%)
  between operations  0.9 us (4%)
    ppermute x2, starting transfers between devices, swap(): return lax.ppermute(block, 'space', pairs + [(j, i) for i, j in pairs])  4.96 us
    pallas_call x1, Pallas kernels, branch(): pl.pallas_call(functools.partial(own_kernel, plane), out_shape=(shape((ti...  4.69 us
    ppermute x2, starting transfers between devices, fetch(): return lax.ppermute(block, 'space', [((i + away) % n, i) for i in range(n)])  3.38 us
    pallas_call x1, Pallas kernels, shards(): pl.pallas_call(functools.partial(join_kernel, plane), out_shape=shape((ti...  2.47 us
    pallas_call x1, Pallas kernels, shards(): pl.pallas_call(functools.partial(prep_kernel, plane), out_shape=(shape((T...  1.71 us
    unnamed x10, local copies, waits for them, and re-layouts  1.38 us
    pallas_call x1, Pallas kernels, shards(): pl.pallas_call(final_kernel, out_shape=shape(state.shape, f32), in_specs=...  0.89 us
  transfers between devices with their start and end apart: 5, of which 0 were waited for; matrix products, arithmetic and copies ran while one was open for 0% of the time, Pallas kernels for 43%

profile of v1, /device:TPU:3, one launch (start us, length us, event | category | flops | bytes accessed | tf_op | source)
XLA Modules:
  0.0 20.5 jit_solution(15768248291047631831)
XLA Ops:
  0.0 0.0 collective-permute-start.62
  0.0 1.7 %prep.1 = (f32[80,256]{1,0:T(8,128)S(1)}, f32[160,128]{1,0:T(8,128)S(1)}, f32[160,128]{1,0:T(8,128)S(1)}, s32[1]{0:T(128)}) custom-call(f32[1,5,64,512]{3,2,1,0:T(8,128)} %state.3, s32[1,256]{1,0:T(1,128)} %pairs.1), custom_call_target="tpu_custom_call" | custom-call | tf_op jit(solution)/shard_map/prep/pallas_call | solution.py:356
  1.7 0.0 copy-start.19
  2.4 0.0 copy-start.20
  2.4 0.0 copy-start.1
  2.4 0.0 copy-done
  2.4 0.0 copy-done.19
  2.4 0.6 %copy-done.20 = f32[512]{0:T(512)S(1)} copy-done((f32[512]{0:T(512)S(1)}, f32[512]{0:T(512)}, u32[]{:S(2)}) %copy-start.20) | copy-done | bytes 2072
  3.1 0.0 copy-done.1
  3.1 13.1 %conditional.1 = (f32[80,256]{1,0:T(8,128)}, f32[80,256]{1,0:T(8,128)}, f32[160,128]{1,0:T(8,128)}, f32[160,128]{1,0:T(8,128)}, f32[4,5,64,128]{3,2,1,0:T(8,128)...) conditional(s32[]{:T(128)} %bitcast, ...), branch_computations={%region_0.0_spmd, %region_1.0_spmd, %region_2.0_spmd, %region_3.0_... | conditional | flops 2147483648 | bytes 5554436 | solution.py:422
  3.1 2.5 %collective-permute-start.31 = (f32[80,256]{1,0:T(8,128)S(1)}, f32[80,256]{1,0:T(8,128)}, u32[]{:S(2)}, u32[]{:S(2)}) collective-permute-start(f32[80,256]{1,0:T(8,128)S(1)} %get-tuple-element.565), channel_id=1, source_target_pairs={{8,0},{9,1},{10,2},{11,3},{12,4},{13,5},{14,6},{15,7},{0,8},{1,9},... | collective-permute-start | bytes 245768 | tf_op jit(solution)/shard_map/cond/branch_8_fun/ppermute | solution.py:378
  5.6 0.9 %collective-permute-start.32 = (f32[80,256]{1,0:T(8,128)S(1)}, f32[80,256]{1,0:T(8,128)}, u32[]{:S(2)}, u32[]{:S(2)}) collective-permute-start(f32[80,256]{1,0:T(8,128)S(1)} %get-tuple-element.565), channel_id=1, source_target_pairs={{9,0},{10,1},{11,2},{12,3},{13,4},{14,5},{15,6},{0,7},{1,8},{2,9},... | collective-permute-start | bytes 245768 | tf_op jit(solution)/shard_map/cond/branch_8_fun/ppermute | solution.py:378
  6.5 1.5 %collective-permute-start.33 = (f32[160,128]{1,0:T(8,128)S(1)}, f32[160,128]{1,0:T(8,128)}, u32[]{:S(2)}, u32[]{:S(2)}) collective-permute-start(f32[160,128]{1,0:T(8,128)S(1)} %get-tuple-element.566), channel_id=1, source_target_pairs={{1,2},{3,4},{5,6},{7,8},{9,10},{11,12},{13,14},{15,0},{2,1},{4,3},... | collective-permute-start | bytes 245768 | tf_op jit(solution)/shard_map/cond/branch_8_fun/ppermute | solution.py:384
  8.0 3.5 %collective-permute-start.34 = (f32[160,128]{1,0:T(8,128)S(1)}, f32[160,128]{1,0:T(8,128)}, u32[]{:S(2)}, u32[]{:S(2)}) collective-permute-start(f32[160,128]{1,0:T(8,128)S(1)} %get-tuple-element.567), channel_id=1, source_target_pairs={{0,1},{2,3},{4,5},{6,7},{8,9},{10,11},{12,13},{14,15},{1,0},{3,2},... | collective-permute-start | bytes 245768 | tf_op jit(solution)/shard_map/cond/branch_8_fun/ppermute | solution.py:384
  11.4 4.7 %own.24 = (f32[4,5,64,128]{3,2,1,0:T(8,128)S(1)}, f32[6,4,80,128]{3,2,1,0:T(8,128)S(1)}, f32[8,128]{1,0:T(8,128)S(1)}, f32[3,512]{1,0:T(4,128)S(1)}, s32[1,256]{1,0:T(1,128)S(1)}) custom-call(f32[1,5,64,512]{3,2,1,0:T(8,128)S(1)} %get-tuple-element.568.state, s32[6,512]{1,0:T(8,128)S(1)} %copy-done.11, f32[1,512]{1,0:T(1,128)S(1)} %get-tuple-element.570.metric, ...), custom_call_target="tpu_custom_call" | custom-call | flops 2147483648 | bytes 4194304 | tf_op jit(solution)/shard_map/cond/branch_8_fun/own/pallas_call | solution.py:389
  16.1 0.0 collective-permute-done.31
  16.2 0.0 collective-permute-done.32
  16.2 0.0 collective-permute-done.33
  16.2 0.0 collective-permute-done.34
  16.2 0.0 copy-start.2
  16.2 0.7 %copy-done.2 = s32[6,512]{1,0:T(8,128)S(1)} copy-done((s32[6,512]{1,0:T(8,128)S(1)}, s32[6,512]{1,0:T(8,128)}, u32[]{:S(2)}) %copy-start.2) | copy-done | bytes 12312
  16.9 2.5 %join.1.partial = f32[4,5,64,128]{3,2,1,0:T(8,128)S(1)} custom-call(f32[1,5,64,512]{3,2,1,0:T(8,128)S(1)} %copy-done, s32[6,512]{1,0:T(8,128)S(1)} %copy-done.2, f32[3,512]{1,0:T(4,128)S(1)} %get-tuple-element.726.weights, f32[8,128]{1,0:T(8,128)S(1)} %get-tuple-element.727.frame, s32[1,256]{1,0:T(1,128)S(1)} %get-tuple-element.728.places, ...), custom_call_target="tpu_custom_call" | custom-call | flops 2147483648 | bytes 4194304 | tf_op jit(solution)/shard_map/join/pallas_call | solution.py:430
  19.4 0.0 collective-permute-done.62.refs_0_
  19.4 0.9 %final.1 = f32[1,5,64,512]{3,2,1,0:T(8,128)} custom-call(f32[4,5,64,128]{3,2,1,0:T(8,128)S(1)} %join.1.partial, f32[3,512]{1,0:T(4,128)S(1)} %get-tuple-element.726.weights, f32[1,5,64,512]{3,2,1,0:T(8,128)S(1)} %collective-permute-done.62.refs_0_), custom_call_target="tpu_custom_call" | custom-call | tf_op jit(solution)/shard_map/final/pallas_call | solution.py:449
  (3 shorter events, 0.0 us)
Async XLA Ops:
  0.0 2.4 %copy-start = (f32[1,5,64,512]{3,2,1,0:T(8,128)S(1)}, f32[1,5,64,512]{3,2,1,0:T(8,128)}, u32[]{:S(2)}) copy-start(f32[1,5,64,512]{3,2,1,0:T(8,128)} %state.3) | copy-start | bytes 1966084
  0.0 19.4 %collective-permute-start.62 = (f32[1,5,64,512]{3,2,1,0:T(8,128)}, f32[1,5,64,512]{3,2,1,0:T(8,128)S(1)}, u32[]{:S(2)}, u32[]{:S(2)}) collective-permute-start(f32[1,5,64,512]{3,2,1,0:T(8,128)} %state.3), channel_id=1, source_target_pairs={{16,0},{0,16},{17,1},{1,17},{18,2},{2,18},{19,3},{3,19},{20,4},{4,... | collective-permute-start | bytes 1966088 | tf_op jit(solution)/shard_map/ppermute | solution.py:352
  1.7 0.7 %copy-start.19 = (f32[3,5,5]{2,0,1:T(4,128)S(1)}, f32[3,5,5]{2,0,1:T(4,128)}, u32[]{:S(2)}) copy-start(f32[3,5,5]{2,0,1:T(4,128)} %param.28) | copy-start | bytes 904
  2.4 0.7 %copy-start.20 = (f32[512]{0:T(512)S(1)}, f32[512]{0:T(512)}, u32[]{:S(2)}) copy-start(f32[512]{0:T(512)} %param.27) | copy-start | bytes 6148
  2.4 0.7 %copy-start.1 = (s32[1,256]{1,0:T(1,128)S(1)}, s32[1,256]{1,0:T(1,128)}, u32[]{:S(2)}) copy-start(s32[1,256]{1,0:T(1,128)} %pairs.1) | copy-start | bytes 3076
  3.1 8.3 %copy-start.11 = (s32[6,512]{1,0:T(8,128)S(1)}, s32[6,512]{1,0:T(8,128)}, u32[]{:S(2)}) copy-start(s32[6,512]{1,0:T(8,128)} %get-tuple-element.569.neighbours) | copy-start | bytes 36868 | tf_op jit(solution)/shard_map/cond
  3.1 13.1 %collective-permute-start.31 = (f32[80,256]{1,0:T(8,128)S(1)}, f32[80,256]{1,0:T(8,128)}, u32[]{:S(2)}, u32[]{:S(2)}) collective-permute-start(f32[80,256]{1,0:T(8,128)S(1)} %get-tuple-element.565), channel_id=1, source_target_pairs={{8,0},{9,1},{10,2},{11,3},{12,4},{13,5},{14,6},{15,7},{0,8},{1,9},... | collective-permute-start | bytes 245768 | tf_op jit(solution)/shard_map/cond/branch_8_fun/ppermute | solution.py:378
  5.6 10.6 %collective-permute-start.32 = (f32[80,256]{1,0:T(8,128)S(1)}, f32[80,256]{1,0:T(8,128)}, u32[]{:S(2)}, u32[]{:S(2)}) collective-permute-start(f32[80,256]{1,0:T(8,128)S(1)} %get-tuple-element.565), channel_id=1, source_target_pairs={{9,0},{10,1},{11,2},{12,3},{13,4},{14,5},{15,6},{0,7},{1,8},{2,9},... | collective-permute-start | bytes 245768 | tf_op jit(solution)/shard_map/cond/branch_8_fun/ppermute | solution.py:378
  6.5 9.7 %collective-permute-start.33 = (f32[160,128]{1,0:T(8,128)S(1)}, f32[160,128]{1,0:T(8,128)}, u32[]{:S(2)}, u32[]{:S(2)}) collective-permute-start(f32[160,128]{1,0:T(8,128)S(1)} %get-tuple-element.566), channel_id=1, source_target_pairs={{1,2},{3,4},{5,6},{7,8},{9,10},{11,12},{13,14},{15,0},{2,1},{4,3},... | collective-permute-start | bytes 245768 | tf_op jit(solution)/shard_map/cond/branch_8_fun/ppermute | solution.py:384
  8.0 8.2 %collective-permute-start.34 = (f32[160,128]{1,0:T(8,128)S(1)}, f32[160,128]{1,0:T(8,128)}, u32[]{:S(2)}, u32[]{:S(2)}) collective-permute-start(f32[160,128]{1,0:T(8,128)S(1)} %get-tuple-element.567), channel_id=1, source_target_pairs={{0,1},{2,3},{4,5},{6,7},{8,9},{10,11},{12,13},{14,15},{1,0},{3,2},... | collective-permute-start | bytes 245768 | tf_op jit(solution)/shard_map/cond/branch_8_fun/ppermute | solution.py:384
  16.2 0.7 %copy-start.2 = (s32[6,512]{1,0:T(8,128)S(1)}, s32[6,512]{1,0:T(8,128)}, u32[]{:S(2)}) copy-start(s32[6,512]{1,0:T(8,128)} %neighbours.1) | copy-start | bytes 36868

commit v2 on v0

--- a/solution.py
+++ b/solution.py
@@ -20,6 +20,7 @@
 VMEM = pl.BlockSpec(memory_space=pltpu.VMEM)
 SMEM = pl.BlockSpec(memory_space=pltpu.SMEM)
 ANY = pl.BlockSpec(memory_space=pl.ANY)
+HBM = pl.BlockSpec(memory_space=pltpu.HBM)
 
 
 def gll_table():
@@ -130,7 +131,7 @@
 def face_weight(mixing, loss, face, g, field):
     sign = 1.0 if face % 2 else -1.0
     value = (3.0 * sign) * mixing[g, face // 2, field]
-    return value - 3.0 * loss[0] if g == field else value
+    return value - 3.0 * loss if g == field else value
 
 
 def base_owner(pairs, plane):
@@ -140,7 +141,10 @@
     return jnp.where(highest - lowest <= 1, lowest, highest)
 
 
-def prep_kernel(plane, state, pairs, rotor, far, near, shift, pairs_here, rim, tiles, sems):
+def prep_kernel(
+    plane, state, pairs, metric, jacobians, rotor, far, near, shift, metric_here, mixing,
+    pairs_here, rim, tiles, sems,
+):
     n = lax.axis_size("space")
     me = lax.axis_index("space")
     count = plane // LANES
@@ -150,7 +154,8 @@
             (state.at[0, :, :, pl.ds(2 * RIM + tile * LANES, LANES)], tiles.at[tile])
             for tile in range(count)
         ]
-        + [(state.at[0, :, :, pl.ds(0, 2 * RIM)], rim)],
+        + [(state.at[0, :, :, pl.ds(0, 2 * RIM)], rim)]
+        + [(metric, metric_here), (jacobians, mixing)],
         sems,
     )
     copies[0].wait()
@@ -161,7 +166,8 @@
             rotor[field * FACE : (field + 1) * FACE, tile_of(tile)] = tiles[
                 tile, field, pl.ds(0, FACE, stride=4), :
             ]
-    copies[-1].wait()
+    for copy in copies[count + 1 :]:
+        copy.wait()
     odd = lax.rem(me, 2) == 1
     lane = lax.broadcasted_iota(jnp.int32, (MODES // 2, 2 * RIM), 1)
     pieces = [
@@ -176,14 +182,10 @@
 
 
 def own_kernel(
-    plane, state, neighbours, metric, jacobians, dissipation, omega, angle, counts, pairs, tables,
-    tendency, outer, given, turned, weights, places,
-    metric_here, mixing, loss, frequency, turn, live_count, pairs_here, table,
+    state, neighbours, jacobians, dissipation, omega, angle, counts, tables,
+    tendency, outer, scalars, mixing, loss, frequency, turn, live_count, table,
     matrix, cells, trace, sems,
 ):
-    n = lax.axis_size("space")
-    inst_count = lax.axis_size("inst")
-    inst = lax.axis_index("inst")
     copies = fetch_all(
         [
             (jacobians, mixing),
@@ -191,90 +193,81 @@
             (omega, frequency),
             (angle, turn),
             (counts, live_count),
-            (metric, metric_here),
-            (pairs, pairs_here),
             (tables, table),
         ],
         sems,
     )
     count = cells.shape[0]
+    elems = state.shape[-1]
 
     for tile in range(count):
         cells[tile] = state[0, :, :, tile_of(tile)]
+    row_number = lax.broadcasted_iota(jnp.int32, (elems, elems), 0)
     for face in range(6):
         for tile in range(count):
-            load_trace(cells, tile, face ^ 1, trace)
-        for tile in range(count):
-            outer[face, tile] = choose(
-                [trace[source] for source in range(count)],
-                neighbours[face : face + 1, tile_of(tile)] - RIM,
-            )
+            load_trace(cells, tile, face ^ 1, trace.at[face])
+        sources = [trace[face, source] for source in range(count)]
+        positions = neighbours[face : face + 1, :] - RIM
+        if face % 2:
+            parts = jnp.concatenate(split(jnp.concatenate(sources, axis=1)), axis=0)
+            matches = jnp.where(row_number == positions, 1.0, 0.0).astype(jnp.bfloat16)
+            found = jnp.dot(parts, matches, preferred_element_type=jnp.float32)
+            for tile in range(count):
+                outer[face, tile] = found[:TRACE, tile_of(tile)] + found[TRACE:, tile_of(tile)]
+        else:
+            for tile in range(count):
+                outer[face, tile] = choose(sources, positions[:, tile_of(tile)])
 
     for copy in copies:
         copy.wait()
+    for row, value in enumerate(
+        [loss[0], frequency[0], turn[0], live_count[0].astype(jnp.float32)]
+    ):
+        scalars[row : row + 1, :] = jnp.full((1, LANES), value)
     lane = lax.broadcasted_iota(jnp.int32, (1, LANES), 1)
-    order = [("high", f) for f in range(FIELDS)] * 2 + [("low", f) for f in range(FIELDS)]
-    order.append(("low", None))
+    layout = [((0, 1), 0, 5), ((2, 3), 1, 6), ((4, 0), 2, 7), ((1, 2), 3, None), ((3, 4), 4, None)]
     for g in range(FIELDS):
-        for pair in range(len(order) // 2):
-            (part, left), (_, right) = order[2 * pair], order[2 * pair + 1]
+        rows = slice(g * MODES, (g + 1) * MODES)
+        values = [
+            [jnp.full((1, LANES), mixing[g, d, field]) for field in range(FIELDS)] for d in range(3)
+        ]
+        for (left, right), high_place, low_place in layout:
             block = None
             for d in range(3):
-                weight = jnp.where(
-                    lane < MODES, mixing[g, d, left], 0.0 if right is None else mixing[g, d, right]
-                )
-                term = weight * table[d]
+                term = jnp.where(lane < MODES, values[d][left], values[d][right]) * table[d]
                 block = term if block is None else block + term
             if g in (left, right):
                 own = lane < MODES if g == left else lane >= MODES
                 block = block + jnp.where(own, loss[0], 0.0) * table[3]
-            if right is None:
-                block = jnp.where(lane < MODES, block, 0.0)
             high, low = split(block)
-            matrix[g * MODES : (g + 1) * MODES, tile_of(pair)] = high if part == "high" else low
-    high, low = split(state[0].reshape(FIELDS * MODES, state.shape[-1]))
+            matrix[rows, tile_of(high_place)] = high
+            if low_place is not None:
+                if left == FIELDS - 1:
+                    low = jnp.where(lane < MODES, low, jnp.zeros_like(low))
+                matrix[rows, tile_of(low_place)] = low
+    high, low = split(state[0].reshape(FIELDS * MODES, elems))
     stacked = jnp.concatenate([high, low, high, jnp.zeros_like(high[:MODES])], axis=0)
     product = jnp.dot(matrix[...], stacked, preferred_element_type=jnp.float32)
     for tile in range(count):
         tendency[tile] = product[:, tile_of(tile)].reshape(FIELDS, MODES, LANES)
 
-    turns = jnp.full((1, LANES), turn[0], jnp.float32)
-    cosine, sine = jnp.cos(turns), jnp.sin(turns)
-    for face in range(6):
-        for g in range(FIELDS):
-            row = (face * FIELDS + g) * FIELDS
-            values = [face_weight(mixing, loss, face, g, field) for field in range(FIELDS)]
-            for field in range(FIELDS):
-                given[row + field : row + field + 1, :] = jnp.full((1, LANES), values[field])
-            if face == 5:
-                values[2], values[3] = (
-                    values[2] * cosine + values[3] * sine,
-                    values[3] * cosine - values[2] * sine,
-                )
-                for field in range(FIELDS):
-                    row = g * FIELDS + field
-                    turned[row : row + 1, :] = jnp.broadcast_to(values[field], (1, LANES))
-
-    spectral = spectral_values(inst_count)
-    scale = metric_here[...]
-    step = COURANT / (scale * loss[0] + frequency[0])
-    live = lax.broadcasted_iota(jnp.int32, scale.shape, 1) < live_count[0]
-    step = jnp.where(live, step, 0.0)
-    weights[0:1, :] = step * scale
-    weights[1:2, :] = jnp.where(live, 1.0, 0.0) - step * (frequency[0] * spectral[0])
-    for away in range(1, inst_count):
-        value = jnp.where(inst + away < inst_count, spectral[-away], spectral[inst_count - away])
-        weights[away + 1 : away + 2, :] = -step * (frequency[0] * value)
-
-    place = pairs_here[...] - base_owner(pairs_here[...], plane) * plane
-    places[...] = jnp.where(place < 0, place + n * plane, place)
+
+def face_weight(mixing, loss, face, g, field):
+    sign = 1.0 if face % 2 else -1.0
+    value = (3.0 * sign) * mixing[g, face // 2, field]
+    return value - 3.0 * loss if g == field else value
 
 
 def halo_kernel(
-    plane, state, neighbours, weights, given, tendency, outer, from_far, from_near,
-    partial, rim, trace,
+    plane, state, metric, jacobians, scalars, neighbours, pairs, tendency, outer,
+    from_far, from_near, partial, weights, turned, places, mixing, rim, trace, sem,
 ):
+    n = lax.axis_size("space")
+    inst_count = lax.axis_size("inst")
+    inst = lax.axis_index("inst")
     count = partial.shape[0]
+    copy = pltpu.make_async_copy(jacobians, mixing, sem)
+    copy.start()
     elems = state.shape[-1]
     odd = lax.rem(lax.axis_index("space"), 2) == 1
     half_lane = lax.broadcasted_iota(jnp.int32, (MODES // 2, 2 * RIM), 1)
@@ -288,34 +281,65 @@
         else:
             left = pltpu.roll(left, RIM, 1)
         rim[0, field, 32 * half : 32 * half + 32, :] = jnp.where(half_lane < RIM, left, right)
+    for face in range(6):
+        load_trace(rim, 0, face ^ 1, trace.at[pl.ds(face, 1)])
+    partial[...] = tendency[...]
+    copy.wait()
+    loss, frequency, turn, live_count = [scalars[row : row + 1, :] for row in range(4)]
     lane = lax.broadcasted_iota(jnp.int32, (1, LANES), 1)
 
-    partial[...] = tendency[...]
     for face in range(6):
-        load_trace(rim, 0, face ^ 1, trace)
+        given = [
+            [face_weight(mixing, loss, face, g, field) for field in range(FIELDS)]
+            for g in range(FIELDS)
+        ]
         for tile in range(count):
             number = neighbours[face : face + 1, tile_of(tile)]
             previous = number < RIM
             remote = previous | (number >= RIM + elems)
-            found = choose([trace[0]], jnp.where(previous, number, number - elems))
+            found = choose([trace[face]], jnp.where(previous, number, number - elems))
             found = jnp.where(remote, found, outer[face, tile])
             if face == 5:
                 column = lane + tile * LANES
                 sliding = (column >= 2 * RIM) & (column < 2 * RIM + plane)
                 found = jnp.where(sliding, 0.0, found)
-            lift(partial, tile, face, mix(given, face, found), 1.0)
+            lift(partial, tile, face, mix(given, found), 1.0)
+
+    spectral = spectral_values(inst_count)
     for tile in range(count):
-        scale, keep = weights[0:1, tile_of(tile)], weights[1:2, tile_of(tile)]
-        partial[tile] = keep * state[0, :, :, tile_of(tile)] + scale * partial[tile]
-
-
-def mix(given, face, found):
+        scale = metric[:, tile_of(tile)]
+        step = COURANT / (scale * loss + frequency)
+        live = (lane + tile * LANES).astype(jnp.float32) < live_count
+        step = jnp.where(live, step, 0.0)
+        keep = jnp.where(live, 1.0, 0.0) - step * (frequency * spectral[0])
+        partial[tile] = keep * state[0, :, :, tile_of(tile)] + (step * scale) * partial[tile]
+        weights[0:1, tile_of(tile)] = step * scale
+        for away in range(1, inst_count):
+            value = jnp.where(
+                inst + away < inst_count, spectral[-away], spectral[inst_count - away]
+            )
+            weights[away : away + 1, tile_of(tile)] = -step * (frequency * value)
+
+    cosine, sine = jnp.cos(turn), jnp.sin(turn)
+    for g in range(FIELDS):
+        values = [face_weight(mixing, loss, 5, g, field) for field in range(FIELDS)]
+        values[2], values[3] = (
+            values[2] * cosine + values[3] * sine,
+            values[3] * cosine - values[2] * sine,
+        )
+        for field in range(FIELDS):
+            row = g * FIELDS + field
+            turned[row : row + 1, :] = jnp.broadcast_to(values[field], (1, LANES))
+    place = pairs[...] - base_owner(pairs[...], plane) * plane
+    places[...] = jnp.where(place < 0, place + n * plane, place)
+
+
+def mix(given, found):
     mixed = []
-    for g in range(FIELDS):
+    for row in given:
         total = None
         for field in range(FIELDS):
-            row = (face * FIELDS + g) * FIELDS + field
-            term = given[row : row + 1, :] * found[field * FACE : (field + 1) * FACE]
+            term = row[field] * found[field * FACE : (field + 1) * FACE]
             total = term if total is None else total + term
         mixed.append(total)
     return mixed
@@ -338,7 +362,7 @@
         for field in range(FIELDS):
             total = partial[tile, field]
             for away in range(1, inst_count):
-                row = weights[away + 1 : away + 2, tile_of(tile)]
+                row = weights[away : away + 1, tile_of(tile)]
                 total = total + row * others[away - 1][0, field, :, tile_of(tile)]
             buffer[tile, field] = total
         if start <= tile < stop:
@@ -351,7 +375,11 @@
                 ],
                 positions,
             )
-            lift(buffer, tile, 5, mix(turned, 0, found), weights[0:1, tile_of(tile)])
+            given = [
+                [turned[row : row + 1, :] for row in range(g * FIELDS, (g + 1) * FIELDS)]
+                for g in range(FIELDS)
+            ]
+            lift(buffer, tile, 5, mix(given, found), weights[0:1, tile_of(tile)])
         copies.append(
             pltpu.make_async_copy(
                 buffer.at[tile], result.at[0, :, :, pl.ds(tile * LANES, LANES)], sems.at[tile]
@@ -372,9 +400,9 @@
     inst_count = lax.axis_size("inst")
     f32 = jnp.float32
     shape = jax.ShapeDtypeStruct
-    mixing = jnp.transpose(jacobians, (1, 0, 2))
     sems = pltpu.SemaphoreType.DMA
     scalar = pltpu.SMEM((1,), f32)
+    mixing_here = pltpu.SMEM((FIELDS, 3, FIELDS), f32)
     params = pltpu.CompilerParams(vmem_limit_bytes=32 * 2**20)
 
     others = [
@@ -382,24 +410,26 @@
         for away in range(1, inst_count)
     ]
 
-    rotor, far, near, shift = pl.pallas_call(
+    rotor, far, near, shift, metric_row, mixing, pairs_row = pl.pallas_call(
         functools.partial(prep_kernel, plane),
         out_shape=(
             shape((TRACE, plane), f32),
             shape((FIELDS * MODES // 2, 2 * RIM), f32),
             shape((FIELDS * MODES // 2, 2 * RIM), f32),
             shape((1,), jnp.int32),
+            shape((1, elems), f32),
+            shape((FIELDS, 3, FIELDS), f32),
+            shape((1, plane), jnp.int32),
         ),
-        in_specs=[ANY, ANY],
-        out_specs=(VMEM, VMEM, VMEM, SMEM),
+        in_specs=[HBM] * 4,
+        out_specs=(VMEM, VMEM, VMEM, SMEM, VMEM, VMEM, VMEM),
         scratch_shapes=[
-            pltpu.VMEM((1, plane), jnp.int32),
             pltpu.VMEM((FIELDS, MODES, 2 * RIM), f32),
             pltpu.VMEM((plane // LANES, FIELDS, MODES, LANES), f32),
-            sems((plane // LANES + 2,)),
+            sems((plane // LANES + 4,)),
         ],
         name="prep",
-    )(state, mortar_pairs)
+    )(state, mortar_pairs, metric.reshape(1, elems), jnp.transpose(jacobians, (1, 0, 2)))
 
     def fetch(away, block):
         if away == 0:
@@ -416,30 +446,25 @@
         first = fetch(away, rotor)
         from_far, from_near = swap(ends, far), swap(middles, near)
         own = pl.pallas_call(
-            functools.partial(own_kernel, plane),
+            own_kernel,
             out_shape=(
                 shape((tiles, FIELDS, MODES, LANES), f32),
                 shape((6, tiles, TRACE, LANES), f32),
-                shape((6 * FIELDS * FIELDS, LANES), f32),
-                shape((FIELDS * FIELDS, LANES), f32),
-                shape((inst_count + 1, elems), f32),
-                shape((1, plane), jnp.int32),
+                shape((8, LANES), f32),
             ),
-            in_specs=[VMEM, VMEM] + [ANY] * 8,
-            out_specs=(VMEM,) * 6,
+            in_specs=[VMEM] * 3 + [HBM] * 5,
+            out_specs=(VMEM,) * 3,
             scratch_shapes=[
-                pltpu.VMEM((1, elems), f32),
-                pltpu.SMEM((FIELDS, 3, FIELDS), f32),
+                mixing_here,
                 scalar,
                 scalar,
                 scalar,
                 pltpu.SMEM((1,), jnp.int32),
-                pltpu.VMEM((1, plane), jnp.int32),
                 pltpu.VMEM((4, MODES, LANES), f32),
                 pltpu.VMEM((FIELDS * MODES, 8 * LANES), jnp.bfloat16),
                 pltpu.VMEM((tiles, FIELDS, MODES, LANES), f32),
-                pltpu.VMEM((tiles, TRACE, LANES), f32),
-                sems((8,)),
+                pltpu.VMEM((6, tiles, TRACE, LANES), f32),
+                sems((6,)),
             ],
             compiler_params=params,
             cost_estimate=pl.CostEstimate(
@@ -449,28 +474,37 @@
         )(*operands)
         return first, from_far, from_near, own
 
-    first, from_far, from_near, own = lax.switch(
+    first, from_far, from_near, (tendency, outer, scalars) = lax.switch(
         shift[0],
         [functools.partial(branch, away) for away in range(n)],
-        rotor, far, near, state, neighbours, metric.reshape(1, elems), mixing, dissipation, omega,
-        rotor_angle, counts, mortar_pairs, jnp.asarray(operator_tables()),
+        rotor, far, near, state, neighbours, mixing, dissipation, omega, rotor_angle, counts,
+        jnp.asarray(operator_tables()),
     )
-    tendency, outer, given, turned, weights, places = own
     second = fetch(1, first)
 
-    partial = pl.pallas_call(
+    partial, weights, turned, places = pl.pallas_call(
         functools.partial(halo_kernel, plane),
-        out_shape=shape((tiles, FIELDS, MODES, LANES), f32),
-        in_specs=[VMEM] * 8,
-        out_specs=VMEM,
+        out_shape=(
+            shape((tiles, FIELDS, MODES, LANES), f32),
+            shape((inst_count, elems), f32),
+            shape((FIELDS * FIELDS, LANES), f32),
+            shape((1, plane), jnp.int32),
+        ),
+        in_specs=[VMEM] * 10,
+        out_specs=(VMEM,) * 4,
         scratch_shapes=[
+            mixing_here,
             pltpu.VMEM((1, FIELDS, MODES, 2 * RIM), f32),
-            pltpu.VMEM((1, TRACE, LANES), f32),
+            pltpu.VMEM((6, TRACE, LANES), f32),
+            sems,
         ],
         compiler_params=params,
         cost_estimate=pl.CostEstimate(flops=2**31, bytes_accessed=2**22, transcendentals=0),
         name="halo",
-    )(state, neighbours, weights, given, tendency, outer, from_far, from_near)
+    )(
+        state, metric_row, mixing, scalars, neighbours, pairs_row, tendency, outer,
+        from_far, from_near,
+    )
 
     return pl.pallas_call(
         functools.partial(final_kernel, plane),

time: 21.4 us -> 22.5 us (1.051); the launches traced: 21.4 us -> 22.8 us
  Pallas kernels: 9.07 us -> 10 us
  loops' own time: 0.27 us -> 1.07 us
  waiting for transfers between devices: 0.38 us -> 0.11 us
    pallas_call x2, Pallas kernels: 6.43 us -> 7.24 us  [the longest x1 4.9 us: branch(): pl.pallas_call(own_kernel, out_shape=(shape((tiles, FIELDS, MODES, LANES)...]
    another operation x1, loops' own time: 0.27 us -> 1.07 us  [shards(): lax.switch(shift[0], [functools.partial(branch, away) for away in range(n...]
    cond x5 -> x1, local copies, waits for them, and re-layouts: 0.69 us -> 0.01 us
    unnamed x6 -> x8, local copies, waits for them, and re-layouts: 0.04 us -> 0.69 us
    ppermute x2, waiting for transfers between devices: 0.38 us -> 0.01 us  [fetch(): return lax.ppermute(block, 'space', [((i + away) % n, i) for i in range(n)])]
  transfers between devices with their start and end apart: 5 -> 5, of which waited for: 1 -> 1; matrix products, arithmetic and copies ran while one was open for 0% -> 0% of each run, Pallas kernels for 38% -> 39%
where the time goes in v2:
time: 22.5 us; the launch traced here: 22.8 us
  starting transfers between devices  10 us (44%)
  Pallas kernels  10 us (44%)
  loops' own time  1.07 us (5%)
  between operations  0.9 us (4%)
  local copies, waits for them, and re-layouts  0.7 us (3%)
    ppermute x2, starting transfers between devices, fetch(): return lax.ppermute(block, 'space', [((i + away) % n, i) for i in range(n)])  5.46 us
    pallas_call x1, Pallas kernels, branch(): pl.pallas_call(own_kernel, out_shape=(shape((tiles, FIELDS, MODES, LANES)...  4.9 us
    ppermute x1, starting transfers between devices, shards(): lax.ppermute(state, 'inst', [((i + away) % inst_count, i) for i in range(...  2.94 us
    pallas_call x1, Pallas kernels, shards(): pl.pallas_call(functools.partial(halo_kernel, plane), out_shape=(shape((t...  2.34 us
    pallas_call x1, Pallas kernels, shards(): pl.pallas_call(functools.partial(prep_kernel, plane), out_shape=(shape((T...  1.75 us
    ppermute x2, starting transfers between devices, swap(): return lax.ppermute(block, 'space', pairs + [(j, i) for i, j in pairs])  1.63 us
    another operation x1, loops' own time, shards(): lax.switch(shift[0], [functools.partial(branch, away) for away in range(n...  1.07 us
    pallas_call x1, Pallas kernels, shards(): pl.pallas_call(functools.partial(final_kernel, plane), out_shape=shape(st...  1.02 us
  transfers between devices with their start and end apart: 5, of which 1 were waited for; matrix products, arithmetic and copies ran while one was open for 0% of the time, Pallas kernels for 39%

profile of v2, /device:TPU:0, one launch (start us, length us, event | category | flops | bytes accessed | tf_op | source)
XLA Modules:
  0.0 22.8 jit_solution(11517465875327605892)
XLA Ops:
  0.0 0.0 copy-start.2
  0.0 2.9 %collective-permute-start.48 = (f32[1,5,64,512]{3,2,1,0:T(8,128)}, f32[1,5,64,512]{3,2,1,0:T(8,128)S(1)}, u32[]{:S(2)}, u32[]{:S(2)}) collective-permute-start(f32[1,5,64,512]{3,2,1,0:T(8,128)} %state.3), channel_id=1, source_target_pairs={{16,0},{0,16},{17,1},{1,17},{18,2},{2,18},{19,3},{3,19},{20,4},{4,... | collective-permute-start | bytes 1966088 | tf_op jit(solution)/shard_map/ppermute | solution.py:409
  2.9 0.0 copy-start.3
  2.9 1.7 %prep.1 = (f32[80,256]{1,0:T(8,128)S(1)}, f32[160,128]{1,0:T(8,128)S(1)}, f32[160,128]{1,0:T(8,128)S(1)}, s32[1]{0:T(128)}, f32[1,512]{1,0:T(1,128)}, /*index=5*/f32[5,3,5]{2,1,0:T(4,128)S(1)}, s32[1,256]{1,0:T(1,128)}) custom-call(f32[1,5,64,512]{3,2,1,0:T(8,128)} %state.3, s32[1,256]{1,0:T(1,128)} %pairs.1, f32[1,512]{1,0:T(1,128)} %bitcast.4, ...), custom_call_target="tpu_custom_call" | custom-call | tf_op jit(solution)/shard_map/prep/pallas_call | solution.py:413
  5.3 0.0 copy-done.2
  5.3 0.0 copy-done.3
  5.4 10.4 %conditional.1 = (f32[80,256]{1,0:T(8,128)S(1)}, f32[160,128]{1,0:T(8,128)}, f32[160,128]{1,0:T(8,128)}, f32[4,5,64,128]{3,2,1,0:T(8,128)S(1)}, f32[6,4,80,128]{3,2,1,0:T(8,128)S(1)}, /*index=5*/f32[8,128]{1,0:T(8,128)S(1)}) conditional(s32[]{:T(128)} %bitcast.2, (f32[160,128]{1,0:T(8,128)S(1)}, ...), branch_computations={%region_0.0_spmd, %region_1.0_spmd, %region_2.0_spmd, %region_3.0_... | conditional | flops 2147483648 | bytes 5341352 | solution.py:477
  5.6 2.7 %collective-permute-start.23 = (f32[80,256]{1,0:T(8,128)S(1)}, f32[80,256]{1,0:T(8,128)S(1)}, u32[]{:S(2)}, u32[]{:S(2)}) collective-permute-start(f32[80,256]{1,0:T(8,128)S(1)} %get-tuple-element.469), channel_id=1, source_target_pairs={{8,0},{9,1},{10,2},{11,3},{12,4},{13,5},{14,6},{15,7},{0,8},{1,9},... | collective-permute-start | bytes 245768 | tf_op jit(solution)/shard_map/cond/branch_8_fun/ppermute | solution.py:437
  8.3 1.2 %collective-permute-start.24 = (f32[160,128]{1,0:T(8,128)S(1)}, f32[160,128]{1,0:T(8,128)}, u32[]{:S(2)}, u32[]{:S(2)}) collective-permute-start(f32[160,128]{1,0:T(8,128)S(1)} %get-tuple-element.470), channel_id=1, source_target_pairs={{1,2},{3,4},{5,6},{7,8},{9,10},{11,12},{13,14},{15,0},{2,1},{4,3},... | collective-permute-start | bytes 245768 | tf_op jit(solution)/shard_map/cond/branch_8_fun/ppermute | solution.py:443
  9.5 0.4 %collective-permute-start.25 = (f32[160,128]{1,0:T(8,128)S(1)}, f32[160,128]{1,0:T(8,128)}, u32[]{:S(2)}, u32[]{:S(2)}) collective-permute-start(f32[160,128]{1,0:T(8,128)S(1)} %get-tuple-element.471), channel_id=1, source_target_pairs={{0,1},{2,3},{4,5},{6,7},{8,9},{10,11},{12,13},{14,15},{1,0},{3,2},... | collective-permute-start | bytes 245768 | tf_op jit(solution)/shard_map/cond/branch_8_fun/ppermute | solution.py:443
  9.9 4.9 %own.24 = (f32[4,5,64,128]{3,2,1,0:T(8,128)S(1)}, f32[6,4,80,128]{3,2,1,0:T(8,128)S(1)}, f32[8,128]{1,0:T(8,128)S(1)}) custom-call(f32[1,5,64,512]{3,2,1,0:T(8,128)S(1)} %get-tuple-element.472.state, s32[6,512]{1,0:T(8,128)S(1)} %get-tuple-element.473.neighbours, f32[5,3,5]{2,1,0:T(4,128)S(1)} %get-tuple-element.474.jacobians, ...), custom_call_target="tpu_custom_call" | custom-call | flops 2147483648 | bytes 4194304 | tf_op jit(solution)/shard_map/cond/branch_8_fun/own/pallas_call | solution.py:448
  14.8 0.0 collective-permute-done.23
  14.9 0.1 collective-permute-done.24
  15.0 0.0 collective-permute-done.25
  15.7 2.8 %collective-permute-start.47 = (f32[80,256]{1,0:T(8,128)S(1)}, f32[80,256]{1,0:T(8,128)S(1)}, u32[]{:S(2)}, u32[]{:S(2)}) collective-permute-start(f32[80,256]{1,0:T(8,128)S(1)} %get-tuple-element.614.first), channel_id=1, source_target_pairs={{1,0},{2,1},{3,2},{4,3},{5,4},{6,5},{7,6},{8,7},{9,8},{10,9},{11,1... | collective-permute-start | bytes 245768 | tf_op jit(solution)/shard_map/ppermute | solution.py:437
  18.5 0.0 copy-start
  18.5 0.0 copy-start.1
  18.5 0.7 %copy-done = f32[1,512]{1,0:T(1,128)S(1)} copy-done((f32[1,512]{1,0:T(1,128)S(1)}, f32[1,512]{1,0:T(1,128)}, u32[]{:S(2)}) %copy-start) | copy-done | bytes 2072
  19.2 0.0 copy-done.1
  19.2 2.3 %halo.1 = (f32[4,5,64,128]{3,2,1,0:T(8,128)S(1)}, f32[2,512]{1,0:T(2,128)S(1)}, f32[25,128]{1,0:T(8,128)S(1)}, s32[1,256]{1,0:T(1,128)S(1)}) custom-call(f32[1,5,64,512]{3,2,1,0:T(8,128)S(1)} %copy-done.2, f32[1,512]{1,0:T(1,128)S(1)} %copy-done, f32[5,3,5]{2,1,0:T(4,128)S(1)} %get-tuple-element.599.jacobians, f32[8,128]{1,0:T(8,128)S(1)} %get-tuple-element.604.scalars, ...), custom_call_target="tpu_custom_call" | custom-call | flops 2147483648 | bytes 4194304 | tf_op jit(solution)/shard_map/halo/pallas_call | solution.py:485
  21.6 0.0 collective-permute-done.47.second
  21.6 0.0 collective-permute-done.48.refs_0_
  21.6 1.0 %final.1 = f32[1,5,64,512]{3,2,1,0:T(8,128)} custom-call(f32[4,5,64,128]{3,2,1,0:T(8,128)S(1)} %get-tuple-element.610.partial, f32[2,512]{1,0:T(2,128)S(1)} %get-tuple-element.611.weights, f32[25,128]{1,0:T(8,128)S(1)} %get-tuple-element.612.turned, s32[1,256]{1,0:T(1,128)S(1)} %get-tuple-element.613.places, f32[80,256]{1,0:T(8,128)S(1)} %get-tuple-element.614.first, ...), custom_call_target="tpu_custom_call" | custom-call | tf_op jit(solution)/shard_map/final/pallas_call | solution.py:509
  (1 shorter events, 0.0 us)
Async XLA Ops:
  0.0 5.3 %copy-start.2 = (f32[1,5,64,512]{3,2,1,0:T(8,128)S(1)}, f32[1,5,64,512]{3,2,1,0:T(8,128)}, u32[]{:S(2)}) copy-start(f32[1,5,64,512]{3,2,1,0:T(8,128)} %state.3) | copy-start | bytes 1966084
  0.0 21.6 %collective-permute-start.48 = (f32[1,5,64,512]{3,2,1,0:T(8,128)}, f32[1,5,64,512]{3,2,1,0:T(8,128)S(1)}, u32[]{:S(2)}, u32[]{:S(2)}) collective-permute-start(f32[1,5,64,512]{3,2,1,0:T(8,128)} %state.3), channel_id=1, source_target_pairs={{16,0},{0,16},{17,1},{1,17},{18,2},{2,18},{19,3},{3,19},{20,4},{4,... | collective-permute-start | bytes 1966088 | tf_op jit(solution)/shard_map/ppermute | solution.py:409
  2.9 2.4 %copy-start.3 = (s32[6,512]{1,0:T(8,128)S(1)}, s32[6,512]{1,0:T(8,128)}, u32[]{:S(2)}) copy-start(s32[6,512]{1,0:T(8,128)} %neighbours.1) | copy-start | bytes 36868
  5.6 9.2 %collective-permute-start.23 = (f32[80,256]{1,0:T(8,128)S(1)}, f32[80,256]{1,0:T(8,128)S(1)}, u32[]{:S(2)}, u32[]{:S(2)}) collective-permute-start(f32[80,256]{1,0:T(8,128)S(1)} %get-tuple-element.469), channel_id=1, source_target_pairs={{8,0},{9,1},{10,2},{11,3},{12,4},{13,5},{14,6},{15,7},{0,8},{1,9},... | collective-permute-start | bytes 245768 | tf_op jit(solution)/shard_map/cond/branch_8_fun/ppermute | solution.py:437
  8.3 6.7 %collective-permute-start.24 = (f32[160,128]{1,0:T(8,128)S(1)}, f32[160,128]{1,0:T(8,128)}, u32[]{:S(2)}, u32[]{:S(2)}) collective-permute-start(f32[160,128]{1,0:T(8,128)S(1)} %get-tuple-element.470), channel_id=1, source_target_pairs={{1,2},{3,4},{5,6},{7,8},{9,10},{11,12},{13,14},{15,0},{2,1},{4,3},... | collective-permute-start | bytes 245768 | tf_op jit(solution)/shard_map/cond/branch_8_fun/ppermute | solution.py:443
  9.5 5.5 %collective-permute-start.25 = (f32[160,128]{1,0:T(8,128)S(1)}, f32[160,128]{1,0:T(8,128)}, u32[]{:S(2)}, u32[]{:S(2)}) collective-permute-start(f32[160,128]{1,0:T(8,128)S(1)} %get-tuple-element.471), channel_id=1, source_target_pairs={{0,1},{2,3},{4,5},{6,7},{8,9},{10,11},{12,13},{14,15},{1,0},{3,2},... | collective-permute-start | bytes 245768 | tf_op jit(solution)/shard_map/cond/branch_8_fun/ppermute | solution.py:443
  15.7 5.8 %collective-permute-start.47 = (f32[80,256]{1,0:T(8,128)S(1)}, f32[80,256]{1,0:T(8,128)S(1)}, u32[]{:S(2)}, u32[]{:S(2)}) collective-permute-start(f32[80,256]{1,0:T(8,128)S(1)} %get-tuple-element.614.first), channel_id=1, source_target_pairs={{1,0},{2,1},{3,2},{4,3},{5,4},{6,5},{7,6},{8,7},{9,8},{10,9},{11,1... | collective-permute-start | bytes 245768 | tf_op jit(solution)/shard_map/ppermute | solution.py:437
  18.5 0.7 %copy-start = (f32[1,512]{1,0:T(1,128)S(1)}, f32[1,512]{1,0:T(1,128)}, u32[]{:S(2)}) copy-start(f32[1,512]{1,0:T(1,128)} %get-tuple-element.598.metric) | copy-start | bytes 6148
  18.5 0.7 %copy-start.1 = (s32[1,256]{1,0:T(1,128)S(1)}, s32[1,256]{1,0:T(1,128)}, u32[]{:S(2)}) copy-start(s32[1,256]{1,0:T(1,128)} %get-tuple-element.605.pairs) | copy-start | bytes 3076
